TPU v7x, 32 devices: a whole 2x2x4 slice. The times are simulated.
32 devices in a mesh: groups: 2 (over x), tm: 8 (over z, y), rows: 2 (over core).
Axes of the slice: x: 2, y: 2, z: 4, core: 2. Of those that a mesh axis runs over, the one named last changes fastest.
Arguments:
- frames_in: bfloat16 [4, 8, 16, 256, 128], P('groups', 'tm', 'rows'), parts along dimension 0, may hold values from -12 to 12
- gain_one: float32 [128], replicated, may hold values from 0.25 to 1.75
- norm_bias_one: float32 [128], replicated, may hold values from -3 to 3
- kernel_one: bfloat16 [3, 3, 3, 128, 128], replicated, may hold values from -0.109375 to 0.109375
- bias_one: float32 [128], replicated, may hold values from -2 to 2
- gain_two: float32 [128], replicated, may hold values from 0.25 to 1.75
- norm_bias_two: float32 [128], replicated, may hold values from -3 to 3
- kernel_two: bfloat16 [3, 3, 3, 128, 128], replicated, may hold values from -0.109375 to 0.109375
- bias_two: float32 [128], replicated, may hold values from -2 to 2
- kernel_down: bfloat16 [3, 3, 128, 128], replicated, may hold values from -0.1875 to 0.1875
- bias_down: float32 [128], replicated, may hold values from -2 to 2
Outputs:
- features_down: bfloat16 [4, 8, 8, 128, 128], P('groups', 'tm', 'rows'), parts along dimension 0
There are 2 independent parts, one for each index of `groups`. A program takes and returns all parts, laid end to end along the dimension named above; an argument that names none is the same for every part. Nothing has to cross between parts.
All inputs are finite; a program needn't handle non-finite values.
Results may differ from a plain program's by a relative error of at most 0.0095.
Values may be sent and summed in bfloat16 or wider, within the bound.
A program may use at most 128 MiB of HBM per device.

v0:
```python
import jax
import jax.numpy as jnp
from jax import lax
from jax.experimental import pallas as pl
from jax.experimental.pallas import tpu as pltpu
from jax.sharding import PartitionSpec as P

G = 32


EPSILON = 1e-06

MESH = pl.DeviceIdType.MESH


def build(batch, height, width, channels, steps, bands):
    half = height // 2
    quarter = width // 2
    C = channels

    def kernel(
        x_ref, scales_ref, k1_ref, k2_ref, kd_ref, out_ref,
        field, weights, down, hidden, paired, spread, sums, others,
        k_sem, own2_sem, own1_sem, relay_sem, in2_sem, in1_sem,
        edge_out, edge_in, sums_out, sums_in, res_out, res_in,
    ):
        t = lax.axis_index("tm")
        r = lax.axis_index("rows")
        has1 = t >= 1
        has2 = t >= 2
        odd = lax.rem(t, 2) == 1
        sends2 = t + 2 < steps
        sends1 = jnp.logical_and(
            t + 1 < steps, jnp.logical_or(jnp.logical_not(odd), t + 2 >= steps)
        )
        relays = jnp.logical_and(odd, has2)
        slots = [jnp.maximum(f, 2 - t) for f in range(3)]
        present = [has2, has1, None]

        loads = []
        for cv, k_ref in enumerate((k1_ref, k2_ref)):
            for a in range(3):
                for b in range(3):
                    for o in range(2):
                        loads.append(
                            (
                                k_ref.at[a, b],
                                weights.at[
                                    cv,
                                    pl.ds((a + o) * 3 * C, 3 * C),
                                    pl.ds((o * 3 + b) * C, C),
                                ],
                            )
                        )
        conv_loads = len(loads) // 2
        for a in range(3):
            for b in range(3):
                loads.append(
                    (
                        kd_ref.at[a, b],
                        down.at[
                            pl.ds(a * 2 * C + (C if b == 1 else 0), C),
                            pl.ds(C if b == 2 else 0, C),
                        ],
                    )
                )
        loads = [
            pltpu.make_async_copy(src, dst, k_sem.at[n])
            for n, (src, dst) in enumerate(loads)
        ]
        for load in loads:
            load.start()

        barrier = pltpu.get_barrier_semaphore()
        expected = bands - 1
        for off in range(1, bands):
            pl.semaphore_signal(
                barrier, inc=1, device_id={"rows": lax.rem(r + off, bands)}, device_id_type=MESH
            )
        for by in (-2, -1, 1, 2):
            there = jnp.logical_and(t + by >= 0, t + by < steps)
            expected = expected + there.astype(jnp.int32)

            @pl.when(there)
            def _():
                pl.semaphore_signal(
                    barrier, inc=1, device_id={"tm": t + by}, device_id_type=MESH
                )

        zero_block = jnp.zeros((3 * C, C), jnp.bfloat16)
        for cv in range(2):
            for b in range(3):
                weights[cv, 9 * C : 12 * C, b * C : (b + 1) * C] = zero_block
                weights[cv, 0 : 3 * C, (3 + b) * C : (4 + b) * C] = zero_block
        for a in range(3):
            down[(2 * a + 1) * C : (2 * a + 2) * C, C : 2 * C] = jnp.zeros((C, C), jnp.bfloat16)

        @pl.when(r == 0)
        def _():
            for cv in range(2):
                for clip in range(batch):
                    for f in range(3):
                        field[cv, clip, f, 0] = jnp.zeros((width, C), jnp.bfloat16)

        @pl.when(r == bands - 1)
        def _():
            for cv in range(2):
                for clip in range(batch):
                    for f in range(3):
                        field[cv, clip, f, height + 1] = jnp.zeros((width, C), jnp.bfloat16)
            for clip in range(batch):
                paired[clip, height] = jnp.zeros((quarter, 2 * C), jnp.bfloat16)

        def rows_of(cv, clip, slot, q):
            return field.at[cv, clip, slot, pl.ds(1 + 2 * q, 2)]

        def own2(cv, clip, q):
            return pltpu.make_async_remote_copy(
                src_ref=rows_of(cv, clip, 2, q), dst_ref=rows_of(cv, clip, 0, q),
                send_sem=own2_sem.at[cv, clip, q], recv_sem=in2_sem.at[cv, clip, q],
                device_id={"tm": t + 2}, device_id_type=MESH,
            )

        def own1(cv, clip, q):
            return pltpu.make_async_remote_copy(
                src_ref=rows_of(cv, clip, 2, q), dst_ref=rows_of(cv, clip, 1, q),
                send_sem=own1_sem.at[cv, clip, q], recv_sem=in1_sem.at[cv, clip, q],
                device_id={"tm": t + 1}, device_id_type=MESH,
            )

        def relay(cv, clip, q):
            return pltpu.make_async_remote_copy(
                src_ref=rows_of(cv, clip, 0, q), dst_ref=rows_of(cv, clip, 1, q),
                send_sem=relay_sem.at[cv, clip, q], recv_sem=in1_sem.at[cv, clip, q],
                device_id={"tm": t - 1}, device_id_type=MESH,
            )

        def edge(cv, clip, slot, way):
            src, dst, by = ((1, height + 1, -1), (height, 0, 1))[way]
            return pltpu.make_async_remote_copy(
                src_ref=field.at[cv, clip, slot, src], dst_ref=field.at[cv, clip, slot, dst],
                send_sem=edge_out.at[cv, clip, slot, way],
                recv_sem=edge_in.at[cv, clip, slot, way],
                device_id={"rows": r + by}, device_id_type=MESH,
            )

        def totals(cv, clip, off):
            return pltpu.make_async_remote_copy(
                src_ref=sums.at[cv, clip], dst_ref=others.at[cv, clip, off - 1],
                send_sem=sums_out.at[cv, clip, off - 1], recv_sem=sums_in.at[cv, clip, off - 1],
                device_id={"rows": lax.rem(r + off, bands)}, device_id_type=MESH,
            )

        def below(clip):
            return pltpu.make_async_remote_copy(
                src_ref=paired.at[clip, 0], dst_ref=paired.at[clip, height],
                send_sem=res_out.at[clip], recv_sem=res_in.at[clip],
                device_id={"rows": r - 1}, device_id_type=MESH,
            )

        def when(condition, action):
            if condition is None:
                action()
            else:
                pl.when(condition)(action)

        def both(first, second):
            return second if first is None else jnp.logical_and(first, second)

        upper = r > 0
        lower = r < bands - 1

        def start_edges(cv, clip, slot):
            when(both(present[slot], upper), lambda: edge(cv, clip, slot, 0).start())
            when(both(present[slot], lower), lambda: edge(cv, clip, slot, 1).start())

        def wait_edges(cv, clip, slot):
            when(both(present[slot], lower), lambda: edge(cv, clip, slot, 0).wait_recv())
            when(both(present[slot], upper), lambda: edge(cv, clip, slot, 1).wait_recv())

        def folded(values):
            return jnp.sum(values.reshape(width // 8, 8, C), axis=0)

        def start_totals(cv, clip, total, square):
            sums[cv, clip, 0:8] = total
            sums[cv, clip, 8:16] = square
            for off in range(1, bands):
                totals(cv, clip, off).start()

        lane = lax.broadcasted_iota(jnp.int32, (1, C), 1)
        size = C // G

        def grouped(values):
            result = values
            for k in range(1, size):
                left = pltpu.roll(values, k, 1)
                right = pltpu.roll(values, C - k, 1)
                result = result + jnp.where(lax.rem(lane, size) >= k, left, 0.0)
                result = result + jnp.where(lax.rem(lane, size) < size - k, right, 0.0)
            return result

        def constants(cv, clip):
            total = sums[cv, clip]
            for off in range(1, bands):
                totals(cv, clip, off).wait_recv()
                total = total + others[cv, clip, off - 1]
            entries = height * bands * width * size
            sum1 = jnp.broadcast_to(jnp.sum(total[0:8], axis=0, keepdims=True), (8, C))
            sum2 = jnp.broadcast_to(jnp.sum(total[8:16], axis=0, keepdims=True), (8, C))
            average = grouped(sum1)[0:1] / entries
            mean_square = grouped(sum2)[0:1] / entries
            inverse = lax.rsqrt(mean_square - average * average + EPSILON)
            return average, inverse * scales_ref[3 * cv : 3 * cv + 1], scales_ref[3 * cv + 1 : 3 * cv + 2]

        def normalize(cv, clip, source):
            average, scale, shift = constants(cv, clip)

            def step(q, _):
                for i in range(2):
                    v = source[clip, 2 * q + i].astype(jnp.float32)
                    s = 0.5 * ((v - average) * scale + shift)
                    field[cv, clip, 2, 1 + 2 * q + i] = (s + s * jnp.tanh(s)).astype(jnp.bfloat16)
                when(sends2, lambda: own2(cv, clip, q).start())
                when(sends1, lambda: own1(cv, clip, q).start())
                return 0

            lax.fori_loop(0, half, step, 0)
            start_edges(cv, clip, 2)

        def receive(cv, clip):
            def second(q, _):
                own2(cv, clip, q).wait_recv()
                when(relays, lambda: relay(cv, clip, q).start())
                return 0

            def first(q, _):
                own1(cv, clip, q).wait_recv()
                return 0

            @pl.when(has2)
            def _():
                lax.fori_loop(0, half, second, 0)

            start_edges(cv, clip, 0)

            @pl.when(has1)
            def _():
                lax.fori_loop(0, half, first, 0)

            start_edges(cv, clip, 1)
            for slot in (2, 0, 1):
                wait_edges(cv, clip, slot)

        column = lax.broadcasted_iota(jnp.int32, (width, 1), 0)

        def convolved(cv, clip, p):
            x = jnp.concatenate(
                [field[cv, clip, slots[f], 2 * p + d] for d in range(4) for f in range(3)], axis=1
            )
            dot = lambda a, b: jnp.dot(a, b, preferred_element_type=jnp.float32)
            y0 = dot(x[:, : 9 * C], weights[cv, : 9 * C, : 2 * C])
            y1 = dot(x, weights[cv, :, 2 * C : 4 * C])
            y2 = dot(x[:, 3 * C :], weights[cv, 3 * C :, 4 * C :])
            bias = scales_ref[3 * cv + 2 : 3 * cv + 3]

            def joined(left, middle, right):
                left = jnp.where(column >= 1, pltpu.roll(left, 1, 0), 0.0)
                right = jnp.where(column < width - 1, pltpu.roll(right, width - 1, 0), 0.0)
                return middle + left + right + bias

            return (
                joined(y0[:, :C], y0[:, C:], y1[:, :C]),
                joined(y1[:, C:], y2[:, :C], y2[:, C:]),
            )

        def conv_one(clip):
            def step(p, carry):
                total, square = carry
                for i, y in enumerate(convolved(0, clip, p)):
                    y = y.astype(jnp.bfloat16)
                    hidden[clip, 2 * p + i] = y
                    y = y.astype(jnp.float32)
                    total = total + folded(y)
                    square = square + folded(y * y)
                return total, square

            zero = jnp.zeros((8, C), jnp.float32)
            start_totals(0 + 1, clip, *lax.fori_loop(0, half, step, (zero, zero)))

        def conv_two(clip):
            def step(p, _):
                for i, y in enumerate(convolved(1, clip, p)):
                    y = y + x_ref[clip, 2 * p + i].astype(jnp.float32)
                    spread[i] = y.astype(jnp.bfloat16).astype(jnp.float32)
                    even = spread[i, pl.ds(0, quarter, stride=2), :]
                    uneven = spread[i, pl.ds(1, quarter, stride=2), :]
                    paired[clip, 2 * p + i] = jnp.concatenate(
                        [even.astype(jnp.bfloat16), uneven.astype(jnp.bfloat16)], axis=1
                    )
                return 0

            step(0, 0)
            when(upper, lambda: below(clip).start())
            lax.fori_loop(1, half, step, 0)

        narrow = lax.broadcasted_iota(jnp.int32, (quarter, 1), 0)

        def downsample(clip):
            when(lower, lambda: below(clip).wait_recv())
            for i in range(half):
                x = jnp.concatenate([paired[clip, 2 * i + a] for a in range(3)], axis=1)
                y = jnp.dot(x, down[...], preferred_element_type=jnp.float32)
                right = pltpu.roll(y[:, C:], quarter - 1, 0)
                y = y[:, :C] + jnp.where(narrow < quarter - 1, right, 0.0) + scales_ref[6:7]
                out_ref[clip, i] = y.astype(jnp.bfloat16)

        for clip in range(batch):
            def gather(i, carry):
                v = x_ref[clip, i].astype(jnp.float32)
                return carry[0] + folded(v), carry[1] + folded(v * v)

            zero = jnp.zeros((8, C), jnp.float32)
            found = lax.fori_loop(0, height, gather, (zero, zero))
            if clip == 0:
                pl.semaphore_wait(barrier, expected)
            start_totals(0, clip, *found)
        for clip in range(batch):
            normalize(0, clip, x_ref)
        for load in loads[:conv_loads]:
            load.wait()
        for clip in range(batch):
            receive(0, clip)
            conv_one(clip)
            normalize(1, clip, hidden)
        for load in loads[conv_loads:]:
            load.wait()
        for clip in range(batch):
            receive(1, clip)
            conv_two(clip)
            downsample(clip)

        for cv in range(2):
            for clip in range(batch):
                def leave(q, _):
                    when(sends2, lambda: own2(cv, clip, q).wait_send())
                    when(sends1, lambda: own1(cv, clip, q).wait_send())
                    when(relays, lambda: relay(cv, clip, q).wait_send())
                    return 0

                lax.fori_loop(0, half, leave, 0)
                for slot in range(3):
                    when(both(present[slot], upper), lambda: edge(cv, clip, slot, 0).wait_send())
                    when(both(present[slot], lower), lambda: edge(cv, clip, slot, 1).wait_send())
                for off in range(1, bands):
                    totals(cv, clip, off).wait_send()
        for clip in range(batch):
            when(upper, lambda: below(clip).wait_send())

    vmem = pl.BlockSpec(memory_space=pltpu.VMEM)
    hbm = pl.BlockSpec(memory_space=pl.ANY)
    dma = pltpu.SemaphoreType.DMA
    return pl.pallas_call(
        kernel,
        out_shape=jax.ShapeDtypeStruct((batch, half, quarter, C), jnp.bfloat16),
        in_specs=[vmem, vmem, hbm, hbm, hbm],
        out_specs=vmem,
        scratch_shapes=[
            pltpu.VMEM((2, batch, 3, height + 2, width, C), jnp.bfloat16),
            pltpu.VMEM((2, 12 * C, 6 * C), jnp.bfloat16),
            pltpu.VMEM((6 * C, 2 * C), jnp.bfloat16),
            pltpu.VMEM((batch, height, width, C), jnp.bfloat16),
            pltpu.VMEM((batch, height + 1, quarter, 2 * C), jnp.bfloat16),
            pltpu.VMEM((2, width, C), jnp.float32),
            pltpu.VMEM((2, batch, 16, C), jnp.float32),
            pltpu.VMEM((2, batch, max(bands - 1, 1), 16, C), jnp.float32),
            dma((45,)),
            dma((2, batch, half)),
            dma((2, batch, half)),
            dma((2, batch, half)),
            dma((2, batch, half)),
            dma((2, batch, half)),
            dma((2, batch, 3, 2)),
            dma((2, batch, 3, 2)),
            dma((2, batch, max(bands - 1, 1))),
            dma((2, batch, max(bands - 1, 1))),
            dma((batch,)),
            dma((batch,)),
        ],
        compiler_params=pltpu.CompilerParams(
            collective_id=0, has_side_effects=True, vmem_limit_bytes=50 * 1024 * 1024
        ),
    )


def solution(mesh):
    steps, bands = mesh.shape["tm"], mesh.shape["rows"]

    def local(
        frames_in,
        gain_one,
        norm_bias_one,
        kernel_one,
        bias_one,
        gain_two,
        norm_bias_two,
        kernel_two,
        bias_two,
        kernel_down,
        bias_down,
    ):
        inputs = frames_in[:, 0]
        batch, height, width, channels = inputs.shape
        scales = jnp.stack(
            [gain_one, norm_bias_one, bias_one, gain_two, norm_bias_two, bias_two, bias_down, bias_down]
        )
        wide = (3, 3, 3 * channels, channels)
        call = build(batch, height, width, channels, steps, bands)
        result = call(
            inputs, scales, kernel_one.reshape(wide), kernel_two.reshape(wide), kernel_down
        )
        return result[:, None]

    placed = (P("groups", "tm", "rows", None, None),) + (P(),) * 10
    return jax.shard_map(
        local,
        mesh=mesh,
        in_specs=placed,
        out_specs=P("groups", "tm", "rows", None, None),
        check_vma=False,
    )
```

profile of v0, /device:TPU:25, one launch (start us, length us, event | category | flops | bytes accessed | tf_op | source)
XLA Modules:
  0.0 70.6 jit_solution(16758853508334129229)
XLA Ops:
  0.0 0.0 copy-start.7
  0.0 0.0 copy-start.8
  0.0 0.0 copy-start.9
  0.0 0.0 copy-start.10
  0.0 0.0 copy-start.4
  0.0 0.0 copy-start.5
  0.0 0.0 copy-start.6
  0.0 0.6 copy-done.7
  0.7 0.0 copy-done.8
  0.7 0.0 copy-done.9
  0.7 0.0 copy-done.10
  0.7 0.0 copy-done.4
  0.7 0.0 copy-done.5
  0.7 0.0 copy-done.6
  0.8 0.0 copy-start
  0.8 1.2 %copy-done = bf16[2,1,8,256,128]{4,3,2,1,0:T(8,128)(2,1)S(1)} copy-done((bf16[2,1,8,256,128]{4,3,2,1,0:T(8,128)(2,1)S(1)}, bf16[2,1,8,256,128]{4,3,2,1,0:T(8,128)(2,1)}, u32[]{:S(2)}) %copy-start) | copy-done | bytes 1048600
  2.0 0.0 copy-start.1
  2.0 1.2 %copy-done.1 = bf16[3,3,3,128,128]{4,3,2,1,0:T(8,128)(2,1)S(1)} copy-done((bf16[3,3,3,128,128]{4,3,2,1,0:T(8,128)(2,1)S(1)}, bf16[3,3,3,128,128]{4,3,2,1,0:T(8,128)(2,1)}, u32[]{:S(2)}) %copy-start.1) | copy-done | bytes 884760
  3.2 0.0 copy-start.2
  3.2 1.2 %copy-done.2 = bf16[3,3,3,128,128]{4,3,2,1,0:T(8,128)(2,1)S(1)} copy-done((bf16[3,3,3,128,128]{4,3,2,1,0:T(8,128)(2,1)S(1)}, bf16[3,3,3,128,128]{4,3,2,1,0:T(8,128)(2,1)}, u32[]{:S(2)}) %copy-start.2) | copy-done | bytes 884760
  4.3 0.0 copy-start.3
  4.3 1.0 %copy-done.3 = bf16[3,3,128,128]{3,2,1,0:T(8,128)(2,1)S(1)} copy-done((bf16[3,3,128,128]{3,2,1,0:T(8,128)(2,1)S(1)}, bf16[3,3,128,128]{3,2,1,0:T(8,128)(2,1)}, u32[]{:S(2)}) %copy-start.3) | copy-done | bytes 294936
  5.3 64.6 %shard_map.109 = bf16[2,4,128,128]{3,2,1,0:T(8,128)(2,1)S(1)} custom-call(bf16[2,8,256,128]{3,2,1,0:T(8,128)(2,1)S(1)} %bitcast.14, f32[8,128]{1,0:T(8,128)S(1)} %stack.32.scales_ref, bf16[3,3,384,128]{3,2,1,0:T(8,128)(2,1)S(1)} %bitcast.15, bf16[3,3,384,128]{3,2,1,0:T(8,128)(2,1)S(1)} %bitcast.16, bf16[3,3,128,128]{3,2,1,0:T(8,128)(2,1)S(1)} %copy-done.3), custom_call_target="tpu_custom_call" | custom-call | tf_op jit(solution)/shard_map/pallas_call | solution.py:418
  69.9 0.7 copy.14
  (1 shorter events, 0.0 us)
Async XLA Ops:
  0.0 0.7 copy-start.7
  0.0 0.7 copy-start.8
  0.0 0.7 copy-start.9
  0.0 0.7 copy-start.10
  0.0 0.7 copy-start.4
  0.0 0.7 copy-start.5
  0.0 0.7 %copy-start.6 = (f32[128]{0:T(128)S(1)}, f32[128]{0:T(128)}, u32[]{:S(2)}) copy-start(f32[128]{0:T(128)} %param.13) | copy-start | bytes 1540
  0.8 1.2 %copy-start = (bf16[2,1,8,256,128]{4,3,2,1,0:T(8,128)(2,1)S(1)}, bf16[2,1,8,256,128]{4,3,2,1,0:T(8,128)(2,1)}, u32[]{:S(2)}) copy-start(bf16[2,1,8,256,128]{4,3,2,1,0:T(8,128)(2,1)} %param.11) | copy-start | bytes 3145732
  2.0 1.2 %copy-start.1 = (bf16[3,3,3,128,128]{4,3,2,1,0:T(8,128)(2,1)S(1)}, bf16[3,3,3,128,128]{4,3,2,1,0:T(8,128)(2,1)}, u32[]{:S(2)}) copy-start(bf16[3,3,3,128,128]{4,3,2,1,0:T(8,128)(2,1)} %param.14) | copy-start | bytes 2654212
  3.2 1.2 %copy-start.2 = (bf16[3,3,3,128,128]{4,3,2,1,0:T(8,128)(2,1)S(1)}, bf16[3,3,3,128,128]{4,3,2,1,0:T(8,128)(2,1)}, u32[]{:S(2)}) copy-start(bf16[3,3,3,128,128]{4,3,2,1,0:T(8,128)(2,1)} %param.18) | copy-start | bytes 2654212
  4.3 1.0 %copy-start.3 = (bf16[3,3,128,128]{3,2,1,0:T(8,128)(2,1)S(1)}, bf16[3,3,128,128]{3,2,1,0:T(8,128)(2,1)}, u32[]{:S(2)}) copy-start(bf16[3,3,128,128]{3,2,1,0:T(8,128)(2,1)} %kd_ref.1) | copy-start | bytes 884740
where the time goes:
time: 70.9 us; the launch traced here: 70.6 us
  Pallas kernels  64.6 us (91%)
  local copies, waits for them, and re-layouts  5.96 us (8%)
    pallas_call x1, Pallas kernels, local(): call(inputs, scales, kernel_one.reshape(wide), kernel_two.reshape(wide),...  64.6 us
    unnamed x23, local copies, waits for them, and re-layouts  5.93 us

commit v1 on v0

--- a/solution.py
+++ b/solution.py
@@ -19,9 +19,10 @@
     C = channels
 
     def kernel(
-        x_ref, scales_ref, k1_ref, k2_ref, kd_ref, out_ref,
-        field, weights, down, hidden, paired, spread, sums, others,
-        k_sem, own2_sem, own1_sem, relay_sem, in2_sem, in1_sem,
+        frames_ref, g1_ref, n1_ref, c1_ref, g2_ref, n2_ref, c2_ref, cd_ref,
+        k1_ref, k2_ref, kd_ref, out_ref,
+        x_ref, scales, field, weights, down, hidden, paired, spread, sums, others,
+        x_sem, scale_sem, k_sem, own2_sem, own1_sem, relay_sem, in2_sem, in1_sem,
         edge_out, edge_in, sums_out, sums_in, res_out, res_in,
     ):
         t = lax.axis_index("tm")
@@ -34,8 +35,24 @@
             t + 1 < steps, jnp.logical_or(jnp.logical_not(odd), t + 2 >= steps)
         )
         relays = jnp.logical_and(odd, has2)
+        inner = r > 0
+
+        def place(i):
+            return jnp.where(inner, i, half - 1 - i)
+
         slots = [jnp.maximum(f, 2 - t) for f in range(3)]
         present = [has2, has1, None]
+
+        frames = [
+            pltpu.make_async_copy(frames_ref.at[clip], x_ref.at[clip], x_sem.at[clip])
+            for clip in range(batch)
+        ]
+        vectors = [
+            pltpu.make_async_copy(ref, scales.at[n], scale_sem.at[n])
+            for n, ref in enumerate((g1_ref, n1_ref, c1_ref, g2_ref, n2_ref, c2_ref, cd_ref))
+        ]
+        for copy in frames + vectors:
+            copy.start()
 
         loads = []
         for cv, k_ref in enumerate((k1_ref, k2_ref)):
@@ -210,12 +227,13 @@
             average = grouped(sum1)[0:1] / entries
             mean_square = grouped(sum2)[0:1] / entries
             inverse = lax.rsqrt(mean_square - average * average + EPSILON)
-            return average, inverse * scales_ref[3 * cv : 3 * cv + 1], scales_ref[3 * cv + 1 : 3 * cv + 2]
+            return average, inverse * scales[3 * cv], scales[3 * cv + 1]
 
         def normalize(cv, clip, source):
             average, scale, shift = constants(cv, clip)
 
-            def step(q, _):
+            def step(n, _):
+                q = place(n)
                 for i in range(2):
                     v = source[clip, 2 * q + i].astype(jnp.float32)
                     s = 0.5 * ((v - average) * scale + shift)
@@ -227,29 +245,39 @@
             lax.fori_loop(0, half, step, 0)
             start_edges(cv, clip, 2)
 
-        def receive(cv, clip):
-            def second(q, _):
+        def arrive(cv, clip, n):
+            q = place(n)
+
+            @pl.when(has2)
+            def _():
                 own2(cv, clip, q).wait_recv()
                 when(relays, lambda: relay(cv, clip, q).start())
-                return 0
-
-            def first(q, _):
-                own1(cv, clip, q).wait_recv()
-                return 0
-
-            @pl.when(has2)
-            def _():
-                lax.fori_loop(0, half, second, 0)
-
-            start_edges(cv, clip, 0)
 
             @pl.when(has1)
             def _():
-                lax.fori_loop(0, half, first, 0)
-
-            start_edges(cv, clip, 1)
+                own1(cv, clip, q).wait_recv()
+
+        def open_edges(cv, clip):
+            early = 1 if bands <= 2 else half
+            for n in range(early):
+                arrive(cv, clip, n)
+            for slot in (0, 1):
+                start_edges(cv, clip, slot)
             for slot in (2, 0, 1):
                 wait_edges(cv, clip, slot)
+            return early
+
+        def pairs(cv, clip, body, carry):
+            early = open_edges(cv, clip)
+
+            def step(n, carry):
+                @pl.when(jnp.logical_and(n < half, n >= early))
+                def _():
+                    arrive(cv, clip, n)
+
+                return body(place(n - 1), n, carry)
+
+            return lax.fori_loop(1, half + 1, step, carry)
 
         column = lax.broadcasted_iota(jnp.int32, (width, 1), 0)
 
@@ -261,7 +289,7 @@
             y0 = dot(x[:, : 9 * C], weights[cv, : 9 * C, : 2 * C])
             y1 = dot(x, weights[cv, :, 2 * C : 4 * C])
             y2 = dot(x[:, 3 * C :], weights[cv, 3 * C :, 4 * C :])
-            bias = scales_ref[3 * cv + 2 : 3 * cv + 3]
+            bias = scales[3 * cv + 2]
 
             def joined(left, middle, right):
                 left = jnp.where(column >= 1, pltpu.roll(left, 1, 0), 0.0)
@@ -274,7 +302,7 @@
             )
 
         def conv_one(clip):
-            def step(p, carry):
+            def step(p, n, carry):
                 total, square = carry
                 for i, y in enumerate(convolved(0, clip, p)):
                     y = y.astype(jnp.bfloat16)
@@ -285,10 +313,10 @@
                 return total, square
 
             zero = jnp.zeros((8, C), jnp.float32)
-            start_totals(0 + 1, clip, *lax.fori_loop(0, half, step, (zero, zero)))
+            start_totals(1, clip, *pairs(0, clip, step, (zero, zero)))
 
         def conv_two(clip):
-            def step(p, _):
+            def step(p, n, _):
                 for i, y in enumerate(convolved(1, clip, p)):
                     y = y + x_ref[clip, 2 * p + i].astype(jnp.float32)
                     spread[i] = y.astype(jnp.bfloat16).astype(jnp.float32)
@@ -297,22 +325,32 @@
                     paired[clip, 2 * p + i] = jnp.concatenate(
                         [even.astype(jnp.bfloat16), uneven.astype(jnp.bfloat16)], axis=1
                     )
+
+                @pl.when(jnp.logical_and(upper, n == 1))
+                def _():
+                    below(clip).start()
+
                 return 0
 
-            step(0, 0)
-            when(upper, lambda: below(clip).start())
-            lax.fori_loop(1, half, step, 0)
+            pairs(1, clip, step, 0)
 
         narrow = lax.broadcasted_iota(jnp.int32, (quarter, 1), 0)
 
         def downsample(clip):
             when(lower, lambda: below(clip).wait_recv())
+            x = jnp.concatenate(
+                [
+                    jnp.concatenate([paired[clip, 2 * i + a] for a in range(3)], axis=1)
+                    for i in range(half)
+                ],
+                axis=0,
+            )
+            y = jnp.dot(x, down[...], preferred_element_type=jnp.float32)
             for i in range(half):
-                x = jnp.concatenate([paired[clip, 2 * i + a] for a in range(3)], axis=1)
-                y = jnp.dot(x, down[...], preferred_element_type=jnp.float32)
-                right = pltpu.roll(y[:, C:], quarter - 1, 0)
-                y = y[:, :C] + jnp.where(narrow < quarter - 1, right, 0.0) + scales_ref[6:7]
-                out_ref[clip, i] = y.astype(jnp.bfloat16)
+                rows = y[i * quarter : (i + 1) * quarter]
+                right = pltpu.roll(rows[:, C:], quarter - 1, 0)
+                rows = rows[:, :C] + jnp.where(narrow < quarter - 1, right, 0.0) + scales[6]
+                out_ref[clip, i] = rows.astype(jnp.bfloat16)
 
         for clip in range(batch):
             def gather(i, carry):
@@ -320,22 +358,23 @@
                 return carry[0] + folded(v), carry[1] + folded(v * v)
 
             zero = jnp.zeros((8, C), jnp.float32)
+            frames[clip].wait()
             found = lax.fori_loop(0, height, gather, (zero, zero))
             if clip == 0:
                 pl.semaphore_wait(barrier, expected)
             start_totals(0, clip, *found)
+        for vector in vectors:
+            vector.wait()
         for clip in range(batch):
             normalize(0, clip, x_ref)
         for load in loads[:conv_loads]:
             load.wait()
         for clip in range(batch):
-            receive(0, clip)
             conv_one(clip)
             normalize(1, clip, hidden)
         for load in loads[conv_loads:]:
             load.wait()
         for clip in range(batch):
-            receive(1, clip)
             conv_two(clip)
             downsample(clip)
 
@@ -362,9 +401,11 @@
     return pl.pallas_call(
         kernel,
         out_shape=jax.ShapeDtypeStruct((batch, half, quarter, C), jnp.bfloat16),
-        in_specs=[vmem, vmem, hbm, hbm, hbm],
+        in_specs=[hbm] * 11,
         out_specs=vmem,
         scratch_shapes=[
+            pltpu.VMEM((batch, height, width, C), jnp.bfloat16),
+            pltpu.VMEM((7, 1, C), jnp.float32),
             pltpu.VMEM((2, batch, 3, height + 2, width, C), jnp.bfloat16),
             pltpu.VMEM((2, 12 * C, 6 * C), jnp.bfloat16),
             pltpu.VMEM((6 * C, 2 * C), jnp.bfloat16),
@@ -373,6 +414,8 @@
             pltpu.VMEM((2, width, C), jnp.float32),
             pltpu.VMEM((2, batch, 16, C), jnp.float32),
             pltpu.VMEM((2, batch, max(bands - 1, 1), 16, C), jnp.float32),
+            dma((batch,)),
+            dma((7,)),
             dma((45,)),
             dma((2, batch, half)),
             dma((2, batch, half)),
@@ -387,7 +430,7 @@
             dma((batch,)),
         ],
         compiler_params=pltpu.CompilerParams(
-            collective_id=0, has_side_effects=True, vmem_limit_bytes=50 * 1024 * 1024
+            collective_id=0, has_side_effects=True, vmem_limit_bytes=60 * 1024 * 1024
         ),
     )
 
@@ -410,13 +453,16 @@
     ):
         inputs = frames_in[:, 0]
         batch, height, width, channels = inputs.shape
-        scales = jnp.stack(
-            [gain_one, norm_bias_one, bias_one, gain_two, norm_bias_two, bias_two, bias_down, bias_down]
-        )
+        vectors = [
+            v.reshape(1, channels)
+            for v in (
+                gain_one, norm_bias_one, bias_one, gain_two, norm_bias_two, bias_two, bias_down
+            )
+        ]
         wide = (3, 3, 3 * channels, channels)
         call = build(batch, height, width, channels, steps, bands)
         result = call(
-            inputs, scales, kernel_one.reshape(wide), kernel_two.reshape(wide), kernel_down
+            inputs, *vectors, kernel_one.reshape(wide), kernel_two.reshape(wide), kernel_down
         )
         return result[:, None]
 

time: 70.9 us -> 62.2 us (0.88)
  local copies, waits for them, and re-layouts: 5.96 us -> 1.67 us
  Pallas kernels: 64.6 us -> 60.4 us
    unnamed x23 -> x1, local copies, waits for them, and re-layouts: 5.93 us -> 1.67 us
    pallas_call x1, Pallas kernels: 64.6 us -> 60.4 us  [local(): call(inputs, *vectors, kernel_one.reshape(wide), kernel_two.reshape(wide)...]
where the time goes in v1:
time: 62.2 us; the launch traced here: 62.1 us
  Pallas kernels  60.4 us (97%)
  local copies, waits for them, and re-layouts  1.67 us (3%)
    pallas_call x1, Pallas kernels, local(): call(inputs, *vectors, kernel_one.reshape(wide), kernel_two.reshape(wide)...  60.4 us
    unnamed x1, local copies, waits for them, and re-layouts  1.67 us

profile of v1, /device:TPU:25, one launch (start us, length us, event | category | flops | bytes accessed | tf_op | source)
XLA Modules:
  0.0 62.1 jit_solution(9910209767406308286)
XLA Ops:
  0.0 60.4 %shard_map.109 = bf16[2,4,128,128]{3,2,1,0:T(8,128)(2,1)} custom-call(bf16[2,8,256,128]{3,2,1,0:T(8,128)(2,1)} %bitcast.14, f32[1,128]{1,0:T(1,128)} %bitcast.17, f32[1,128]{1,0:T(1,128)} %bitcast.18, f32[1,128]{1,0:T(1,128)} %bitcast.19, f32[1,128]{1,0:T(1,128)} %bitcast.20, f32[1,128]{1,0:T(1,128)} %bitcast.21, f32[1,128]{1,0:T(1,128)} %bitcast.22, ...), custom_call_target="tpu_custom_call" | custom-call | tf_op jit(solution)/shard_map/pallas_call | solution.py:464
  60.4 1.7 %copy.14 = bf16[2,1,4,128,128]{4,3,2,1,0:T(8,128)(2,1)} copy(bf16[2,1,4,128,128]{4,3,2,1,0:T(8,128)(2,1)} %bitcast.13) | data formatting | bytes 524288

commit v2 on v1

--- a/solution.py
+++ b/solution.py
@@ -21,9 +21,9 @@
     def kernel(
         frames_ref, g1_ref, n1_ref, c1_ref, g2_ref, n2_ref, c2_ref, cd_ref,
         k1_ref, k2_ref, kd_ref, out_ref,
-        x_ref, scales, field, weights, down, hidden, paired, spread, sums, others,
+        x_ref, scales, raw, whole, arrived, settled, field, weights, down, hidden, paired, spread, sums, others,
         x_sem, scale_sem, k_sem, own2_sem, own1_sem, relay_sem, in2_sem, in1_sem,
-        edge_out, edge_in, sums_out, sums_in, res_out, res_in,
+        whole2_sem, whole1_sem, whole_relay_sem, whole_in, edge_out, edge_in, sums_out, sums_in, res_out, res_in,
     ):
         t = lax.axis_index("tm")
         r = lax.axis_index("rows")
@@ -40,8 +40,27 @@
         def place(i):
             return jnp.where(inner, i, half - 1 - i)
 
+        def row_at(n, i):
+            return jnp.where(inner, 2 * n + i, height - 1 - 2 * n - i)
+
         slots = [jnp.maximum(f, 2 - t) for f in range(3)]
         present = [has2, has1, None]
+
+        barrier = pltpu.get_barrier_semaphore()
+        expected = bands - 1
+        for off in range(1, bands):
+            pl.semaphore_signal(
+                barrier, inc=1, device_id={"rows": lax.rem(r + off, bands)}, device_id_type=MESH
+            )
+        for by in (-2, -1, 1, 2):
+            there = jnp.logical_and(t + by >= 0, t + by < steps)
+            expected = expected + there.astype(jnp.int32)
+
+            @pl.when(there)
+            def _():
+                pl.semaphore_signal(
+                    barrier, inc=1, device_id={"tm": t + by}, device_id_type=MESH
+                )
 
         frames = [
             pltpu.make_async_copy(frames_ref.at[clip], x_ref.at[clip], x_sem.at[clip])
@@ -88,22 +107,6 @@
         for load in loads:
             load.start()
 
-        barrier = pltpu.get_barrier_semaphore()
-        expected = bands - 1
-        for off in range(1, bands):
-            pl.semaphore_signal(
-                barrier, inc=1, device_id={"rows": lax.rem(r + off, bands)}, device_id_type=MESH
-            )
-        for by in (-2, -1, 1, 2):
-            there = jnp.logical_and(t + by >= 0, t + by < steps)
-            expected = expected + there.astype(jnp.int32)
-
-            @pl.when(there)
-            def _():
-                pl.semaphore_signal(
-                    barrier, inc=1, device_id={"tm": t + by}, device_id_type=MESH
-                )
-
         zero_block = jnp.zeros((3 * C, C), jnp.bfloat16)
         for cv in range(2):
             for b in range(3):
@@ -128,27 +131,55 @@
             for clip in range(batch):
                 paired[clip, height] = jnp.zeros((quarter, 2 * C), jnp.bfloat16)
 
-        def rows_of(cv, clip, slot, q):
-            return field.at[cv, clip, slot, pl.ds(1 + 2 * q, 2)]
+        def landing(cv, clip, slot, row):
+            if cv == 0:
+                return raw.at[clip, slot, row]
+            return field.at[cv, clip, slot, row + 1]
+
+        def leaving(cv, clip, row):
+            if cv == 0:
+                return frames_ref.at[clip, row]
+            return field.at[cv, clip, 2, row + 1]
 
         def own2(cv, clip, q):
             return pltpu.make_async_remote_copy(
-                src_ref=rows_of(cv, clip, 2, q), dst_ref=rows_of(cv, clip, 0, q),
+                src_ref=leaving(cv, clip, q), dst_ref=landing(cv, clip, 0, q),
                 send_sem=own2_sem.at[cv, clip, q], recv_sem=in2_sem.at[cv, clip, q],
                 device_id={"tm": t + 2}, device_id_type=MESH,
             )
 
         def own1(cv, clip, q):
             return pltpu.make_async_remote_copy(
-                src_ref=rows_of(cv, clip, 2, q), dst_ref=rows_of(cv, clip, 1, q),
+                src_ref=leaving(cv, clip, q), dst_ref=landing(cv, clip, 1, q),
                 send_sem=own1_sem.at[cv, clip, q], recv_sem=in1_sem.at[cv, clip, q],
                 device_id={"tm": t + 1}, device_id_type=MESH,
             )
 
         def relay(cv, clip, q):
             return pltpu.make_async_remote_copy(
-                src_ref=rows_of(cv, clip, 0, q), dst_ref=rows_of(cv, clip, 1, q),
+                src_ref=landing(cv, clip, 0, q), dst_ref=landing(cv, clip, 1, q),
                 send_sem=relay_sem.at[cv, clip, q], recv_sem=in1_sem.at[cv, clip, q],
+                device_id={"tm": t - 1}, device_id_type=MESH,
+            )
+
+        def whole2(clip):
+            return pltpu.make_async_remote_copy(
+                src_ref=whole.at[clip], dst_ref=arrived.at[clip, 0],
+                send_sem=whole2_sem.at[clip], recv_sem=whole_in.at[clip, 0],
+                device_id={"tm": t + 2}, device_id_type=MESH,
+            )
+
+        def whole1(clip):
+            return pltpu.make_async_remote_copy(
+                src_ref=whole.at[clip], dst_ref=arrived.at[clip, 1],
+                send_sem=whole1_sem.at[clip], recv_sem=whole_in.at[clip, 1],
+                device_id={"tm": t + 1}, device_id_type=MESH,
+            )
+
+        def whole_relay(clip):
+            return pltpu.make_async_remote_copy(
+                src_ref=arrived.at[clip, 0], dst_ref=arrived.at[clip, 1],
+                send_sem=whole_relay_sem.at[clip], recv_sem=whole_in.at[clip, 1],
                 device_id={"tm": t - 1}, device_id_type=MESH,
             )
 
@@ -216,64 +247,105 @@
                 result = result + jnp.where(lax.rem(lane, size) < size - k, right, 0.0)
             return result
 
-        def constants(cv, clip):
+        def summed(cv, clip):
             total = sums[cv, clip]
             for off in range(1, bands):
                 totals(cv, clip, off).wait_recv()
                 total = total + others[cv, clip, off - 1]
+            return total
+
+        def constants(cv, total):
             entries = height * bands * width * size
             sum1 = jnp.broadcast_to(jnp.sum(total[0:8], axis=0, keepdims=True), (8, C))
             sum2 = jnp.broadcast_to(jnp.sum(total[8:16], axis=0, keepdims=True), (8, C))
             average = grouped(sum1)[0:1] / entries
             mean_square = grouped(sum2)[0:1] / entries
             inverse = lax.rsqrt(mean_square - average * average + EPSILON)
-            return average, inverse * scales[3 * cv], scales[3 * cv + 1]
-
-        def normalize(cv, clip, source):
-            average, scale, shift = constants(cv, clip)
+            return average, inverse * scales[3 * cv]
+
+        def normed(cv, values, average, scale):
+            s = 0.5 * ((values.astype(jnp.float32) - average) * scale + scales[3 * cv + 1])
+            return (s + s * jnp.tanh(s)).astype(jnp.bfloat16)
+
+        def send(cv, clip, row):
+            when(sends2, lambda: own2(cv, clip, row).start())
+            when(sends1, lambda: own1(cv, clip, row).start())
+
+        def normalize(cv, clip, source, total):
+            average, scale = constants(cv, total)
 
             def step(n, _):
-                q = place(n)
                 for i in range(2):
-                    v = source[clip, 2 * q + i].astype(jnp.float32)
-                    s = 0.5 * ((v - average) * scale + shift)
-                    field[cv, clip, 2, 1 + 2 * q + i] = (s + s * jnp.tanh(s)).astype(jnp.bfloat16)
-                when(sends2, lambda: own2(cv, clip, q).start())
-                when(sends1, lambda: own1(cv, clip, q).start())
+                    row = row_at(n, i)
+                    field[cv, clip, 2, row + 1] = normed(cv, source[clip, row], average, scale)
+                    if cv == 1:
+                        send(cv, clip, row)
                 return 0
 
             lax.fori_loop(0, half, step, 0)
             start_edges(cv, clip, 2)
 
-        def arrive(cv, clip, n):
-            q = place(n)
-
+        def land(cv, clip, n):
             @pl.when(has2)
             def _():
-                own2(cv, clip, q).wait_recv()
-                when(relays, lambda: relay(cv, clip, q).start())
-
-            @pl.when(has1)
-            def _():
-                own1(cv, clip, q).wait_recv()
+                for i in range(2):
+                    row = row_at(n, i)
+                    own2(cv, clip, row).wait_recv()
+                    when(relays, lambda: relay(cv, clip, row).start())
+
+        def settle(cv, clip, n):
+            def take(slot):
+                for i in range(2):
+                    row = row_at(n, i)
+                    if slot == 1:
+                        own1(cv, clip, row).wait_recv()
+                    if cv == 0:
+                        field[cv, clip, slot, row + 1] = normed(
+                            cv, raw[clip, slot, row], settled[slot, 0], settled[slot, 1]
+                        )
+
+            for slot in range(2):
+                when(present[slot], lambda: take(slot))
+
+        def learn(clip):
+            def take(slot):
+                whole_in_copy = (whole2, whole1)[slot](clip)
+                whole_in_copy.wait_recv()
+                if slot == 0:
+                    when(relays, lambda: whole_relay(clip).start())
+                settled[slot, 0], settled[slot, 1] = constants(0, arrived[clip, slot])
+
+            for slot in range(2):
+                when(present[slot], lambda: take(slot))
+
+        lead = min(2, half)
 
         def open_edges(cv, clip):
             early = 1 if bands <= 2 else half
+            ahead = max(early, lead if cv == 0 else 1)
+            for n in range(ahead):
+                land(cv, clip, n)
+            if cv == 0:
+                learn(clip)
             for n in range(early):
-                arrive(cv, clip, n)
+                settle(cv, clip, n)
             for slot in (0, 1):
                 start_edges(cv, clip, slot)
             for slot in (2, 0, 1):
                 wait_edges(cv, clip, slot)
-            return early
+            return early, ahead
 
         def pairs(cv, clip, body, carry):
-            early = open_edges(cv, clip)
+            early, ahead = open_edges(cv, clip)
 
             def step(n, carry):
+                @pl.when(jnp.logical_and(n < half, n >= ahead))
+                def _():
+                    land(cv, clip, n)
+
                 @pl.when(jnp.logical_and(n < half, n >= early))
                 def _():
-                    arrive(cv, clip, n)
+                    settle(cv, clip, n)
 
                 return body(place(n - 1), n, carry)
 
@@ -352,6 +424,16 @@
                 rows = rows[:, :C] + jnp.where(narrow < quarter - 1, right, 0.0) + scales[6]
                 out_ref[clip, i] = rows.astype(jnp.bfloat16)
 
+        def send_frames(clip, first, last):
+            def step(n, _):
+                for i in range(2):
+                    send(0, clip, row_at(n, i))
+                return 0
+
+            lax.fori_loop(first, last, step, 0)
+
+        pl.semaphore_wait(barrier, expected)
+        send_frames(0, 0, lead)
         for clip in range(batch):
             def gather(i, carry):
                 v = x_ref[clip, i].astype(jnp.float32)
@@ -359,19 +441,23 @@
 
             zero = jnp.zeros((8, C), jnp.float32)
             frames[clip].wait()
-            found = lax.fori_loop(0, height, gather, (zero, zero))
-            if clip == 0:
-                pl.semaphore_wait(barrier, expected)
-            start_totals(0, clip, *found)
+            start_totals(0, clip, *lax.fori_loop(0, height, gather, (zero, zero)))
+        for clip in range(batch):
+            if clip > 0:
+                send_frames(clip, 0, lead)
+            whole[clip] = summed(0, clip)
+            when(sends2, lambda: whole2(clip).start())
+            when(sends1, lambda: whole1(clip).start())
+            send_frames(clip, lead, half)
         for vector in vectors:
             vector.wait()
         for clip in range(batch):
-            normalize(0, clip, x_ref)
+            normalize(0, clip, x_ref, whole[clip])
         for load in loads[:conv_loads]:
             load.wait()
         for clip in range(batch):
             conv_one(clip)
-            normalize(1, clip, hidden)
+            normalize(1, clip, hidden, summed(1, clip))
         for load in loads[conv_loads:]:
             load.wait()
         for clip in range(batch):
@@ -386,7 +472,7 @@
                     when(relays, lambda: relay(cv, clip, q).wait_send())
                     return 0
 
-                lax.fori_loop(0, half, leave, 0)
+                lax.fori_loop(0, height, leave, 0)
                 for slot in range(3):
                     when(both(present[slot], upper), lambda: edge(cv, clip, slot, 0).wait_send())
                     when(both(present[slot], lower), lambda: edge(cv, clip, slot, 1).wait_send())
@@ -394,9 +480,12 @@
                     totals(cv, clip, off).wait_send()
         for clip in range(batch):
             when(upper, lambda: below(clip).wait_send())
+            when(sends2, lambda: whole2(clip).wait_send())
+            when(sends1, lambda: whole1(clip).wait_send())
+            when(relays, lambda: whole_relay(clip).wait_send())
 
     vmem = pl.BlockSpec(memory_space=pltpu.VMEM)
-    hbm = pl.BlockSpec(memory_space=pl.ANY)
+    hbm = pl.BlockSpec(memory_space=pltpu.HBM)
     dma = pltpu.SemaphoreType.DMA
     return pl.pallas_call(
         kernel,
@@ -406,6 +495,10 @@
         scratch_shapes=[
             pltpu.VMEM((batch, height, width, C), jnp.bfloat16),
             pltpu.VMEM((7, 1, C), jnp.float32),
+            pltpu.VMEM((batch, 2, height, width, C), jnp.bfloat16),
+            pltpu.VMEM((batch, 16, C), jnp.float32),
+            pltpu.VMEM((batch, 2, 16, C), jnp.float32),
+            pltpu.VMEM((2, 2, 1, C), jnp.float32),
             pltpu.VMEM((2, batch, 3, height + 2, width, C), jnp.bfloat16),
             pltpu.VMEM((2, 12 * C, 6 * C), jnp.bfloat16),
             pltpu.VMEM((6 * C, 2 * C), jnp.bfloat16),
@@ -417,11 +510,15 @@
             dma((batch,)),
             dma((7,)),
             dma((45,)),
-            dma((2, batch, half)),
-            dma((2, batch, half)),
-            dma((2, batch, half)),
-            dma((2, batch, half)),
-            dma((2, batch, half)),
+            dma((2, batch, height)),
+            dma((2, batch, height)),
+            dma((2, batch, height)),
+            dma((2, batch, height)),
+            dma((2, batch, height)),
+            dma((batch,)),
+            dma((batch,)),
+            dma((batch,)),
+            dma((batch, 2)),
             dma((2, batch, 3, 2)),
             dma((2, batch, 3, 2)),
             dma((2, batch, max(bands - 1, 1))),

time: 62.2 us -> 61.9 us (level)
  no operation moved by 1% of the time
where the time goes in v2:
time: 61.9 us; the launch traced here: 61.8 us
  Pallas kernels  60.1 us (97%)
  local copies, waits for them, and re-layouts  1.67 us (3%)
    pallas_call x1, Pallas kernels, local(): call(inputs, *vectors, kernel_one.reshape(wide), kernel_two.reshape(wide)...  60.1 us
    unnamed x1, local copies, waits for them, and re-layouts  1.67 us

profile of v2, /device:TPU:25, one launch (start us, length us, event | category | flops | bytes accessed | tf_op | source)
XLA Modules:
  0.0 61.8 jit_solution(15474807283216994876)
XLA Ops:
  0.0 60.1 %shard_map.109 = bf16[2,4,128,128]{3,2,1,0:T(8,128)(2,1)} custom-call(bf16[2,8,256,128]{3,2,1,0:T(8,128)(2,1)} %bitcast.14, f32[1,128]{1,0:T(1,128)} %bitcast.17, f32[1,128]{1,0:T(1,128)} %bitcast.18, f32[1,128]{1,0:T(1,128)} %bitcast.19, f32[1,128]{1,0:T(1,128)} %bitcast.20, f32[1,128]{1,0:T(1,128)} %bitcast.21, f32[1,128]{1,0:T(1,128)} %bitcast.22, ...), custom_call_target="tpu_custom_call" | custom-call | tf_op jit(solution)/shard_map/pallas_call | solution.py:561
  60.1 1.7 %copy.14 = bf16[2,1,4,128,128]{4,3,2,1,0:T(8,128)(2,1)} copy(bf16[2,1,4,128,128]{4,3,2,1,0:T(8,128)(2,1)} %bitcast.13) | data formatting | bytes 524288

commit v3 on v2

--- a/solution.py
+++ b/solution.py
@@ -323,7 +323,7 @@
         def open_edges(cv, clip):
             early = 1 if bands <= 2 else half
             ahead = max(early, lead if cv == 0 else 1)
-            for n in range(ahead):
+            for n in range(1, ahead):
                 land(cv, clip, n)
             if cv == 0:
                 learn(clip)
@@ -456,12 +456,17 @@
         for load in loads[:conv_loads]:
             load.wait()
         for clip in range(batch):
+            if clip == 0:
+                land(0, 0, 0)
             conv_one(clip)
+            land(*((0, clip + 1) if clip + 1 < batch else (1, 0)), 0)
             normalize(1, clip, hidden, summed(1, clip))
         for load in loads[conv_loads:]:
             load.wait()
         for clip in range(batch):
             conv_two(clip)
+            if clip + 1 < batch:
+                land(1, clip + 1, 0)
             downsample(clip)
 
         for cv in range(2):

time: 61.9 us -> 61 us (0.985)
  Pallas kernels: 60.1 us -> 59.2 us
    pallas_call x1, Pallas kernels: 60.1 us -> 59.2 us  [local(): call(inputs, *vectors, kernel_one.reshape(wide), kernel_two.reshape(wide)...]
where the time goes in v3:
time: 61 us; the launch traced here: 60.9 us
  Pallas kernels  59.2 us (97%)
  local copies, waits for them, and re-layouts  1.67 us (3%)
    pallas_call x1, Pallas kernels, local(): call(inputs, *vectors, kernel_one.reshape(wide), kernel_two.reshape(wide)...  59.2 us
    unnamed x1, local copies, waits for them, and re-layouts  1.67 us

profile of v3, /device:TPU:25, one launch (start us, length us, event | category | flops | bytes accessed | tf_op | source)
XLA Modules:
  0.0 60.9 jit_solution(6441426714708300048)
XLA Ops:
  0.0 59.2 %shard_map.109 = bf16[2,4,128,128]{3,2,1,0:T(8,128)(2,1)} custom-call(bf16[2,8,256,128]{3,2,1,0:T(8,128)(2,1)} %bitcast.14, f32[1,128]{1,0:T(1,128)} %bitcast.17, f32[1,128]{1,0:T(1,128)} %bitcast.18, f32[1,128]{1,0:T(1,128)} %bitcast.19, f32[1,128]{1,0:T(1,128)} %bitcast.20, f32[1,128]{1,0:T(1,128)} %bitcast.21, f32[1,128]{1,0:T(1,128)} %bitcast.22, ...), custom_call_target="tpu_custom_call" | custom-call | tf_op jit(solution)/shard_map/pallas_call | solution.py:566
  59.2 1.7 %copy.14 = bf16[2,1,4,128,128]{4,3,2,1,0:T(8,128)(2,1)} copy(bf16[2,1,4,128,128]{4,3,2,1,0:T(8,128)(2,1)} %bitcast.13) | data formatting | bytes 524288

commit v4 on v3

--- a/solution.py
+++ b/solution.py
@@ -131,15 +131,23 @@
             for clip in range(batch):
                 paired[clip, height] = jnp.zeros((quarter, 2 * C), jnp.bfloat16)
 
+        def size_of(cv, clip):
+            return 1 if (cv, clip) == (1, batch - 1) else 2
+
+        def starts(cv, clip, n):
+            if size_of(cv, clip) == 2:
+                return [2 * place(n)]
+            return [row_at(n, i) for i in range(2)]
+
         def landing(cv, clip, slot, row):
             if cv == 0:
-                return raw.at[clip, slot, row]
-            return field.at[cv, clip, slot, row + 1]
+                return raw.at[clip, slot, pl.ds(row, size_of(cv, clip))]
+            return field.at[cv, clip, slot, pl.ds(row + 1, size_of(cv, clip))]
 
         def leaving(cv, clip, row):
             if cv == 0:
-                return frames_ref.at[clip, row]
-            return field.at[cv, clip, 2, row + 1]
+                return frames_ref.at[clip, pl.ds(row, size_of(cv, clip))]
+            return field.at[cv, clip, 2, pl.ds(row + 1, size_of(cv, clip))]
 
         def own2(cv, clip, q):
             return pltpu.make_async_remote_copy(
@@ -278,7 +286,8 @@
                 for i in range(2):
                     row = row_at(n, i)
                     field[cv, clip, 2, row + 1] = normed(cv, source[clip, row], average, scale)
-                    if cv == 1:
+                if cv == 1:
+                    for row in starts(cv, clip, n):
                         send(cv, clip, row)
                 return 0
 
@@ -288,17 +297,17 @@
         def land(cv, clip, n):
             @pl.when(has2)
             def _():
+                for row in starts(cv, clip, n):
+                    own2(cv, clip, row).wait_recv()
+                    when(relays, lambda: relay(cv, clip, row).start())
+
+        def settle(cv, clip, n):
+            def take(slot):
+                if slot == 1:
+                    for row in starts(cv, clip, n):
+                        own1(cv, clip, row).wait_recv()
                 for i in range(2):
                     row = row_at(n, i)
-                    own2(cv, clip, row).wait_recv()
-                    when(relays, lambda: relay(cv, clip, row).start())
-
-        def settle(cv, clip, n):
-            def take(slot):
-                for i in range(2):
-                    row = row_at(n, i)
-                    if slot == 1:
-                        own1(cv, clip, row).wait_recv()
                     if cv == 0:
                         field[cv, clip, slot, row + 1] = normed(
                             cv, raw[clip, slot, row], settled[slot, 0], settled[slot, 1]
@@ -426,8 +435,8 @@
 
         def send_frames(clip, first, last):
             def step(n, _):
-                for i in range(2):
-                    send(0, clip, row_at(n, i))
+                for row in starts(0, clip, n):
+                    send(0, clip, row)
                 return 0
 
             lax.fori_loop(first, last, step, 0)
@@ -471,13 +480,14 @@
 
         for cv in range(2):
             for clip in range(batch):
-                def leave(q, _):
+                def leave(n, _):
+                    q = n * size_of(cv, clip)
                     when(sends2, lambda: own2(cv, clip, q).wait_send())
                     when(sends1, lambda: own1(cv, clip, q).wait_send())
                     when(relays, lambda: relay(cv, clip, q).wait_send())
                     return 0
 
-                lax.fori_loop(0, height, leave, 0)
+                lax.fori_loop(0, height // size_of(cv, clip), leave, 0)
                 for slot in range(3):
                     when(both(present[slot], upper), lambda: edge(cv, clip, slot, 0).wait_send())
                     when(both(present[slot], lower), lambda: edge(cv, clip, slot, 1).wait_send())

time: 61 us -> 61.5 us (level); the launches traced: 60.9 us -> 60.7 us
  no operation moved by 1% of the time
where the time goes in v4:
time: 61.5 us; the launch traced here: 60.7 us
  Pallas kernels  59.1 us (96%)
  local copies, waits for them, and re-layouts  1.67 us (3%)
    pallas_call x1, Pallas kernels, local(): call(inputs, *vectors, kernel_one.reshape(wide), kernel_two.reshape(wide)...  59.1 us
    unnamed x1, local copies, waits for them, and re-layouts  1.67 us

profile of v4, /device:TPU:25, one launch (start us, length us, event | category | flops | bytes accessed | tf_op | source)
XLA Modules:
  0.0 60.7 jit_solution(4330804943005986652)
XLA Ops:
  0.0 59.1 %shard_map.109 = bf16[2,4,128,128]{3,2,1,0:T(8,128)(2,1)} custom-call(bf16[2,8,256,128]{3,2,1,0:T(8,128)(2,1)} %bitcast.14, f32[1,128]{1,0:T(1,128)} %bitcast.17, f32[1,128]{1,0:T(1,128)} %bitcast.18, f32[1,128]{1,0:T(1,128)} %bitcast.19, f32[1,128]{1,0:T(1,128)} %bitcast.20, f32[1,128]{1,0:T(1,128)} %bitcast.21, f32[1,128]{1,0:T(1,128)} %bitcast.22, ...), custom_call_target="tpu_custom_call" | custom-call | tf_op jit(solution)/shard_map/pallas_call | solution.py:576
  59.1 1.7 %copy.14 = bf16[2,1,4,128,128]{4,3,2,1,0:T(8,128)(2,1)} copy(bf16[2,1,4,128,128]{4,3,2,1,0:T(8,128)(2,1)} %bitcast.13) | data formatting | bytes 524288
